TPU v7x, 512 devices: a whole 4x8x8 slice. The times are simulated.
512 devices in a mesh: dap: 128 (over z_lo, y, x, core), dp: 4 (over z_hi).
Axes of the slice: x: 4, y: 8, z: 8 (z_hi: 4, z_lo: 2; z = z_hi * 2 + z_lo), core: 2. Of those that a mesh axis runs over, the one named last changes fastest.
Arguments:
- pair: bfloat16 [1024, 256, 128], P(('dp', 'dap')), parts along dimension 0, may hold values from -6 to 6
- pair_mask: int32 [1024, 256], P(('dp', 'dap')), parts along dimension 0, may hold values from 0 to 1, as said below
- w_left: bfloat16 [128, 256], replicated, may hold values from -0.5 to 0.5
- w_right: bfloat16 [128, 256], replicated, may hold values from -0.5 to 0.5
- w_tri_gate: bfloat16 [128, 128], replicated, may hold values from -0.5 to 0.5
- w_tri_out: bfloat16 [128, 128], replicated, may hold values from -0.5 to 0.5
- w_attend: bfloat16 [128, 512], replicated, may hold values from -0.5 to 0.5
- w_bias: bfloat16 [128, 4], replicated
- w_att_out: bfloat16 [128, 128], replicated, may hold values from -0.5 to 0.5
Outputs:
- pair_out: float32 [1024, 256, 128], P('dp', 'dap'), parts along dimension 0
There are 4 independent parts, one for each index of `dp`. A program takes and returns all parts, laid end to end along the dimension named above; an argument that names none is the same for every part. Nothing has to cross between parts.
Inputs may be any that keep to these rules, and one draw needn't show every extreme that they name: pair_mask[i, i] = 1 for every residue i.
All inputs are finite; a program needn't handle non-finite values.
Results may differ from a plain program's by a relative error of at most 0.014.
The roundings to bfloat16 on the way count: a program that leaves them out, or rounds other values in their place, can miss the bound.
Values may be sent and summed in bfloat16 or wider, within the bound.
A program may use at most 128 MiB of HBM per device.

v0:
```python
import math
import jax
import jax.numpy as jnp
from jax import lax
from jax.sharding import Mesh
from jax.sharding import PartitionSpec as P

DAP = ("dap_0", "dap_1", "dap_2", "dap_3")
DP_DAP = ("dp", "dap_0", "dap_1", "dap_2", "dap_3")


def from_everyone(value, axis):
    length = lax.axis_size(axis)
    return lax.all_to_all(
        jnp.broadcast_to(value[None], (length, *value.shape)), axis, 0, 0, tiled=True
    )


def joined_along(parts, dim):
    parts = jnp.moveaxis(parts, 0, dim)
    dims = parts.shape
    return parts.reshape(*dims[:dim], dims[dim] * dims[dim + 1], *dims[dim + 2 :])


def whole_of(value, axes, dim):
    far, near = axes
    parts = from_everyone(from_everyone(value, far), near)
    return joined_along(parts.swapaxes(0, 1).reshape(-1, *value.shape), dim)


def in_one_piece(arrays, axis, split_dim, concat_dim, along):
    widths = [math.prod(a.shape[along:]) for a in arrays]
    both = jnp.concatenate(
        [a.reshape(*a.shape[:along], w) for a, w in zip(arrays, widths)], axis=along
    )
    result = lax.all_to_all(both, axis, split_axis=split_dim, concat_axis=concat_dim, tiled=True)
    parts = jnp.split(result, [sum(widths[:k]) for k in range(1, len(widths))], axis=along)
    return tuple(
        (b.reshape(*result.shape[:along], *a.shape[along:]) for a, b in zip(arrays, parts))
    )


def layer_norm(x):
    x = x.astype(jnp.float32)
    mean = jnp.mean(x, axis=-1, keepdims=True)
    var = jnp.mean((x - mean) * (x - mean), axis=-1, keepdims=True)
    return (x - mean) / jnp.sqrt(var + 1e-05)


def matmul(x, w):
    flat = x.reshape(-1, x.shape[-1])
    return jnp.dot(flat, w, preferred_element_type=jnp.float32).reshape(
        x.shape[:-1] + (w.shape[1],)
    )


def edges(zn, weight, maskf, hidden):
    both = matmul(zn, weight)
    return (jax.nn.sigmoid(both[..., :hidden]) * both[..., hidden:] * maskf[..., None]).astype(
        jnp.bfloat16
    )


def triangle_update(pair_part, zn_part, tri, w_tri_gate, w_tri_out):
    tn = layer_norm(tri).astype(jnp.bfloat16)
    update = jax.nn.sigmoid(matmul(zn_part, w_tri_gate)) * matmul(tn, w_tri_out)
    return pair_part.astype(jnp.float32) + update


def attention(pair1, mask_cols, w_attend, w_bias, w_att_out):
    inner = w_att_out.shape[0]
    heads = w_bias.shape[1]
    head_dim = inner // heads
    total, local = (pair1.shape[0], pair1.shape[1])
    yn = layer_norm(pair1).astype(jnp.bfloat16)
    proj = matmul(yn, w_attend)
    query = proj[..., :inner].astype(jnp.bfloat16).reshape(total, local, heads, head_dim)
    keys = proj[..., inner : 2 * inner].astype(jnp.bfloat16).reshape(total, local, heads, head_dim)
    values = (
        proj[..., 2 * inner : 3 * inner].astype(jnp.bfloat16).reshape(total, local, heads, head_dim)
    )
    gate = jax.nn.sigmoid(proj[..., 3 * inner :])
    bias_part = jnp.einsum("kic,ch->hki", yn, w_bias, preferred_element_type=jnp.float32).astype(
        jnp.bfloat16
    )
    bias = whole_of(bias_part, (("dap_0", "dap_1", "dap_2"), "dap_3"), 2)
    scores = jnp.einsum(
        "irhd,krhd->rhki", query, keys, preferred_element_type=jnp.float32
    ) / jnp.sqrt(jnp.float32(head_dim))
    scores = scores + bias.astype(jnp.float32)[None]
    live = jnp.transpose(mask_cols.astype(jnp.float32))[:, None, :, None]
    scores = jnp.where(live > 0.5, scores, jnp.float32(-1000000000.0))
    weights = jax.nn.softmax(scores, axis=2).astype(jnp.bfloat16)
    summed = jnp.einsum(
        "rhki,krhd->irhd", weights, values, preferred_element_type=jnp.float32
    ).reshape(total, local, inner)
    att = (gate * summed).astype(jnp.bfloat16)
    return pair1 + matmul(att, w_att_out)


def shards(pair, pair_mask, w_left, w_right, w_tri_gate, w_tri_out, w_attend, w_bias, w_att_out):
    hidden = w_tri_out.shape[0]
    maskf = pair_mask.astype(jnp.float32)
    zn = layer_norm(pair).astype(jnp.bfloat16)
    left_edge = edges(zn, w_left, maskf, hidden)
    right_edge = edges(zn, w_right, maskf, hidden)
    pair_cols, mask_cols = in_one_piece((pair, pair_mask.astype(jnp.bfloat16)), DAP, 1, 0, 2)
    tri = jnp.einsum(
        "ikc,jkc->ijc",
        lax.all_gather(left_edge, DAP, axis=0, tiled=True),
        right_edge,
        preferred_element_type=jnp.float32,
    )
    zn_cols = layer_norm(pair_cols).astype(jnp.bfloat16)
    pair1 = triangle_update(pair_cols, zn_cols, tri, w_tri_gate, w_tri_out)
    return attention(pair1, mask_cols, w_attend, w_bias, w_att_out)


def solution(mesh):
    torus = Mesh(
        mesh.devices.reshape(2, 8, 4, 2, mesh.shape["dp"]),
        ("dap_0", "dap_1", "dap_2", "dap_3", "dp"),
    )
    placed = (P(DP_DAP, None, None), P(DP_DAP, None), P(), P(), P(), P(), P(), P(), P())
    return jax.shard_map(
        shards, mesh=torus, in_specs=placed, out_specs=P("dp", DAP, None), check_vma=False
    )
```

profile of v0, /device:TPU:1, one launch (start us, length us, event | category | flops | bytes accessed | tf_op | source)
XLA Modules:
  0.0 323.6 jit_solution(5676171652191276352)
XLA Ops:
  6.5 1.1 convert_reduce_fusion.1
  7.6 1.2 fusion.18
  8.8 1.2 fusion.39
  10.0 1.2 fusion.41
  11.3 0.8 fusion.21
  12.1 0.0 all-gather.2.cloned.1.call-update
  12.1 0.1 copy.140
  12.3 0.2 copy.141
  12.5 1.0 pad_maximum_fusion
  13.5 14.2 %all-to-all-start = ((bf16[2,256,129]{2,0,1:T(2,128)(2,1)}), bf16[2,256,129]{2,0,1:T(2,128)(2,1)S(1)}, u32[]{:S(2)}, u32[]{:S(2)}) async-start(bf16[2,256,129]{2,0,1:T(2,128)(2,1)} %pad_maximum_fusion), calls=%async_computation | async-start | bytes 524288 | tf_op jit(solution)/shard_map/all_to_all | solution.py:36
  27.7 0.1 copy.146
  27.9 15.0 %all-to-all-done = bf16[2,256,129]{2,0,1:T(2,128)(2,1)S(1)} async-done(((bf16[2,256,129]{2,0,1:T(2,128)(2,1)}), bf16[2,256,129]{2,0,1:T(2,128)(2,1)S(1)}, u32[]{:S(2)}, u32[]{:S(2)}) %all-to-all-start) | async-done | bytes 132128 | tf_op jit(solution)/shard_map/all_to_all | solution.py:36
  42.8 0.2 copy.142
  43.0 0.1 split.8
  43.1 0.1 split.9
  43.2 0.1 copy.172
  43.4 0.1 copy.174
  43.5 0.1 fusion.16
  43.6 0.0 copy-done.6
  43.6 0.3 fusion.5
  43.9 207.1 %all-gather.2.cloned.1.call-done = bf16[256,256,128]{2,1,0:T(8,128)(2,1)} async-done(((bf16[2,256,128]{2,1,0:T(8,128)(2,1)}), bf16[256,256,128]{2,1,0:T(8,128)(2,1)}) %all-gather.2.cloned.1.call-update) | async-done | bytes 16777232 | tf_op jit(solution)/shard_map/all_gather | solution.py:110
  251.0 22.1 %copy.147 = bf16[256,256,128]{1,0,2:T(8,128)(2,1)} copy(bf16[256,256,128]{2,1,0:T(8,128)(2,1)} %all-gather.2.cloned.1.call-done) | data formatting | bytes 33554432 | tf_op jit(solution)/shard_map/all_gather | solution.py:110
  273.1 10.2 %fusion.58 = (f32[256,2]{0,1:T(2,128)S(1)}, f32[256,2,128]{0,1,2:T(2,128)S(1)}) fusion(bf16[2,256,128]{1,0,2:T(2,128)(2,1)S(1)} %copy.146, bf16[256,256,128]{1,0,2:T(8,128)(2,1)} %copy.147), kind=kOutput, calls=%fused_computation.85 | convolution fusion | flops 33619456 | bytes 17172480 | tf_op jit(solution)/shard_map/ikc,jkc->ijc/dot_general | solution.py:108
  283.4 0.2 multiply_reduce_fusion.1
  283.6 0.1 divide_convert_fusion.3
  283.7 0.0 copy-done.2
  283.7 0.2 fusion.59
  284.1 0.1 fusion.6
  284.2 0.8 broadcast_in_dim.13
  285.0 9.0 %all-to-all-start.1 = ((bf16[64,4,256,2]{2,1,3,0:T(4,128)(2,1)}), bf16[64,4,256,2]{2,1,3,0:T(4,128)(2,1)S(1)}, u32[]{:S(2)}, u32[]{:S(2)}) async-start(bf16[64,4,256,2]{2,1,3,0:T(4,128)(2,1)} %broadcast_in_dim.13), calls=%async_computation.1 | async-start | bytes 524288 | tf_op jit(solution)/shard_map/all_to_all | solution.py:14
  294.0 0.3 fusion.60
  294.4 0.1 fusion.56
  294.4 0.1 copy.154
  294.6 0.1 copy.155
  294.7 0.1 copy.152
  294.9 0.1 copy.173
  295.0 9.8 %all-to-all-done.1 = bf16[64,4,256,2]{2,1,3,0:T(4,128)(2,1)S(1)} async-done(((bf16[64,4,256,2]{2,1,3,0:T(4,128)(2,1)}), bf16[64,4,256,2]{2,1,3,0:T(4,128)(2,1)S(1)}, u32[]{:S(2)}, u32[]{:S(2)}) %all-to-all-start.1) | async-done | bytes 262176 | tf_op jit(solution)/shard_map/all_to_all | solution.py:14
  304.8 0.1 broadcast_in_dim.14
  304.9 7.3 %all_to_all.28 = bf16[2,64,4,256,2]{3,2,4,1,0:T(4,128)(2,1)S(1)} all-to-all(bf16[2,64,4,256,2]{3,2,4,1,0:T(4,128)(2,1)S(1)} %broadcast_in_dim.14), channel_id=1, replica_groups=mesh['dap_0'=2,'dap_1'=8,'dap_2'=4,'dap_3'=2,'dp'=4] {'dap_3'}, dimensions={0} | all-to-all | bytes 1048576 | tf_op jit(solution)/shard_map/all_to_all | solution.py:14
  312.2 0.1 convert_bitcast_fusion
  312.4 0.6 copy.157
  312.9 0.3 copy.158
  313.2 0.4 copy.159
  313.6 0.9 fusion.61
  314.5 1.1 fusion.11
  315.6 0.1 fusion.30
  315.7 0.2 convolution_add_fusion
  316.0 0.8 copy.162
  (27 shorter events, 0.3 us)
Async XLA Ops:
  6.5 287.5 %copy-start = (bf16[128,512]{1,0:T(8,128)(2,1)S(1)}, bf16[128,512]{1,0:T(8,128)(2,1)}, u32[]{:S(2)}) copy-start(bf16[128,512]{1,0:T(8,128)(2,1)} %param.15) | copy-start | bytes 393220
  6.5 5.6 %copy-start.1 = (bf16[2,256,128]{2,1,0:T(8,128)(2,1)S(1)}, bf16[2,256,128]{2,1,0:T(8,128)(2,1)}, u32[]{:S(2)}) copy-start(bf16[2,256,128]{2,1,0:T(8,128)(2,1)} %param.9) | copy-start | bytes 393220
  6.5 4.7 %copy-start.4 = (s32[2,256]{1,0:T(2,128)S(1)}, s32[2,256]{1,0:T(2,128)}, u32[]{:S(2)}) copy-start(s32[2,256]{1,0:T(2,128)} %param.10) | copy-start | bytes 6148
  6.5 244.5 %all-gather.2.cloned.1.call-start = ((), (), s32[]{:S(2)}) async-start(), calls=%async_computation.3 | async-start | bytes 16908288 | tf_op jit(solution)/shard_map/all_gather | solution.py:110
  12.1 31.5 %copy-start.6 = (bf16[128,128]{1,0:T(8,128)(2,1)S(1)}, bf16[128,128]{1,0:T(8,128)(2,1)}, u32[]{:S(2)}) copy-start(bf16[128,128]{1,0:T(8,128)(2,1)} %param.13) | copy-start | bytes 98308
  13.5 29.3 %all-to-all-start = ((bf16[2,256,129]{2,0,1:T(2,128)(2,1)}), bf16[2,256,129]{2,0,1:T(2,128)(2,1)S(1)}, u32[]{:S(2)}, u32[]{:S(2)}) async-start(bf16[2,256,129]{2,0,1:T(2,128)(2,1)} %pad_maximum_fusion), calls=%async_computation | async-start | bytes 524288 | tf_op jit(solution)/shard_map/all_to_all | solution.py:36
  273.1 10.6 %copy-start.2 = (bf16[128,128]{1,0:T(8,128)(2,1)S(1)}, bf16[128,128]{1,0:T(8,128)(2,1)}, u32[]{:S(2)}) copy-start(bf16[128,128]{1,0:T(8,128)(2,1)} %param.14) | copy-start | bytes 98308
  283.3 0.7 copy-start.5
  285.0 19.8 %all-to-all-start.1 = ((bf16[64,4,256,2]{2,1,3,0:T(4,128)(2,1)}), bf16[64,4,256,2]{2,1,3,0:T(4,128)(2,1)S(1)}, u32[]{:S(2)}, u32[]{:S(2)}) async-start(bf16[64,4,256,2]{2,1,3,0:T(4,128)(2,1)} %broadcast_in_dim.13), calls=%async_computation.1 | async-start | bytes 524288 | tf_op jit(solution)/shard_map/all_to_all | solution.py:14
  314.5 1.2 copy-start.3
Sparse Core Ops, SparseCore 0:
  12.3 238.7 all-gather.1
where the time goes:
time: 325 us; the launch traced here: 324 us
  waiting for transfers between devices  232 us (71%)
  local copies, waits for them, and re-layouts  26.8 us (8%)
  starting transfers between devices  23.2 us (7%)
  matrix products  15.9 us (5%)
  between operations  13.7 us (4%)
  blocking collectives  7.31 us (2%)
  other arithmetic  4.84 us (1%)
    all_gather x1, waiting for transfers between devices, shards(): lax.all_gather(left_edge, DAP, axis=0, tiled=True)  207 us
    all_gather x1, local copies, waits for them, and re-layouts, shards(): lax.all_gather(left_edge, DAP, axis=0, tiled=True)  22.1 us
    all_to_all x1, waiting for transfers between devices, in_one_piece(): lax.all_to_all(both, axis, split_axis=split_dim, concat_axis=concat_dim,...  15 us
    all_to_all x1, starting transfers between devices, in_one_piece(): lax.all_to_all(both, axis, split_axis=split_dim, concat_axis=concat_dim,...  14.2 us
    dot_general x1, matrix products, shards(): jnp.einsum('ikc,jkc->ijc', lax.all_gather(left_edge, DAP, axis=0, tiled=T...  10.2 us
    all_to_all x1, waiting for transfers between devices, from_everyone(): lax.all_to_all(jnp.broadcast_to(value[None], (length, *value.shape)), axi...  9.77 us
    all_to_all x1, starting transfers between devices, from_everyone(): lax.all_to_all(jnp.broadcast_to(value[None], (length, *value.shape)), axi...  9.02 us
    all_to_all x1, blocking collectives, from_everyone(): lax.all_to_all(jnp.broadcast_to(value[None], (length, *value.shape)), axi...  7.31 us
  transfers between devices with their start and end apart: 3, of which 3 were waited for; matrix products, arithmetic and copies ran while one was open for 1% of the time, Pallas kernels for 0%

commit v1 on v0

--- a/solution.py
+++ b/solution.py
@@ -7,6 +7,15 @@
 
 DAP = ("dap_0", "dap_1", "dap_2", "dap_3")
 DP_DAP = ("dp", "dap_0", "dap_1", "dap_2", "dap_3")
+
+
+def report_panel(array_dim, q_in):
+    in_order = []
+    for _ in range(jax.lax.axis_size(DAP)):
+        in_order.append(q_in)
+    y_new = jnp.stack(in_order, axis=0)
+    wide_out = jax.lax.all_to_all(y_new, DAP, 0, 0)
+    return jnp.concatenate(wide_out, axis=array_dim)
 
 
 def from_everyone(value, axis):
@@ -106,10 +115,7 @@
     right_edge = edges(zn, w_right, maskf, hidden)
     pair_cols, mask_cols = in_one_piece((pair, pair_mask.astype(jnp.bfloat16)), DAP, 1, 0, 2)
     tri = jnp.einsum(
-        "ikc,jkc->ijc",
-        lax.all_gather(left_edge, DAP, axis=0, tiled=True),
-        right_edge,
-        preferred_element_type=jnp.float32,
+        "ikc,jkc->ijc", report_panel(0, left_edge), right_edge, preferred_element_type=jnp.float32
     )
     zn_cols = layer_norm(pair_cols).astype(jnp.bfloat16)
     pair1 = triangle_update(pair_cols, zn_cols, tri, w_tri_gate, w_tri_out)

time: 325 us -> 503 us (1.55)
  waiting for transfers between devices: 232 us -> 388 us
  local copies, waits for them, and re-layouts: 26.8 us -> 55.1 us
  between operations: 13.7 us -> 0.36 us
  starting transfers between devices: 23.2 us -> 31.3 us
    all_to_all x0 -> x1, waiting for transfers between devices: none -> 367 us  [report_panel(): wide_out = jax.lax.all_to_all(y_new, DAP, 0, 0)]
    all_gather x1 -> x0, waiting for transfers between devices: 207 us -> none  [shards(): lax.all_gather(left_edge, DAP, axis=0, tiled=True)]
    reshape x0 -> x1, local copies, waits for them, and re-layouts: none -> 24.9 us  [report_panel(): return jnp.concatenate(wide_out, axis=array_dim)]
    all_gather x1 -> x0, local copies, waits for them, and re-layouts: 22.1 us -> none  [shards(): lax.all_gather(left_edge, DAP, axis=0, tiled=True)]
    all_to_all x0 -> x1, local copies, waits for them, and re-layouts: none -> 14.4 us  [report_panel(): wide_out = jax.lax.all_to_all(y_new, DAP, 0, 0)]
    another operation x0 -> x1, local copies, waits for them, and re-layouts: none -> 10.2 us  [report_panel(): y_new = jnp.stack(in_order, axis=0)]
    all_to_all x0 -> x1, starting transfers between devices: none -> 7.02 us  [report_panel(): wide_out = jax.lax.all_to_all(y_new, DAP, 0, 0)]
where the time goes in v1:
time: 503 us; the launch traced here: 502 us
  waiting for transfers between devices  388 us (77%)
  local copies, waits for them, and re-layouts  55.1 us (11%)
  starting transfers between devices  31.3 us (6%)
  matrix products  15 us (3%)
  blocking collectives  7.32 us (1%)
    all_to_all x1, waiting for transfers between devices, report_panel(): wide_out = jax.lax.all_to_all(y_new, DAP, 0, 0)  367 us
    reshape x1, local copies, waits for them, and re-layouts, report_panel(): return jnp.concatenate(wide_out, axis=array_dim)  24.9 us
    all_to_all x1, local copies, waits for them, and re-layouts, report_panel(): wide_out = jax.lax.all_to_all(y_new, DAP, 0, 0)  14.4 us
    all_to_all x1, starting transfers between devices, in_one_piece(): lax.all_to_all(both, axis, split_axis=split_dim, concat_axis=concat_dim,...  14.2 us
    all_to_all x1, waiting for transfers between devices, in_one_piece(): lax.all_to_all(both, axis, split_axis=split_dim, concat_axis=concat_dim,...  11 us
    dot_general x1, matrix products, shards(): jnp.einsum('ikc,jkc->ijc', report_panel(0, left_edge), right_edge, prefer...  10.2 us
    another operation x1, local copies, waits for them, and re-layouts, report_panel(): y_new = jnp.stack(in_order, axis=0)  10.2 us
  transfers between devices with their start and end apart: 3, of which 3 were waited for; matrix products, arithmetic and copies ran while one was open for 1% of the time, Pallas kernels for 0%

profile of v1, /device:TPU:1, one launch (start us, length us, event | category | flops | bytes accessed | tf_op | source)
XLA Modules:
  0.0 501.8 jit_solution(2999170607602480266)
XLA Ops:
  0.0 0.8 fusion.57
  0.8 0.2 copy.145
  1.0 1.0 copy.144
  2.0 1.0 pad_maximum_fusion
  3.0 14.2 %all-to-all-start = ((bf16[2,256,129]{2,0,1:T(2,128)(2,1)}), bf16[2,256,129]{2,0,1:T(2,128)(2,1)S(1)}, u32[]{:S(2)}, u32[]{:S(2)}) async-start(bf16[2,256,129]{2,0,1:T(2,128)(2,1)} %pad_maximum_fusion), calls=%async_computation | async-start | bytes 524288 | tf_op jit(solution)/shard_map/all_to_all | solution.py:45
  17.2 1.0 convert_reduce_fusion.1
  18.3 1.2 fusion.18
  19.4 1.2 fusion.39
  20.7 0.3 fusion.41
  21.0 0.2 fusion.21
  21.2 0.1 copy.150
  21.3 11.0 %all-to-all-done = bf16[2,256,129]{2,0,1:T(2,128)(2,1)S(1)} async-done(((bf16[2,256,129]{2,0,1:T(2,128)(2,1)}), bf16[2,256,129]{2,0,1:T(2,128)(2,1)S(1)}, u32[]{:S(2)}, u32[]{:S(2)}) %all-to-all-start) | async-done | bytes 132128 | tf_op jit(solution)/shard_map/all_to_all | solution.py:45
  32.4 10.2 %stack.2 = bf16[128,2,256,128]{2,1,3,0:T(2,128)(2,1)} broadcast(bf16[2,256,128]{1,0,2:T(2,128)(2,1)S(1)} %copy.150), dimensions={1,2,3} | broadcast | bytes 16908288 | tf_op jit(solution)/shard_map/stack | solution.py:16
  42.5 7.0 %all-to-all-start.1 = ((bf16[128,2,256,128]{2,1,3,0:T(2,128)(2,1)}), bf16[128,2,256,128]{2,1,3,0:T(2,128)(2,1)}, u32[]{:S(2)}, u32[]{:S(2)}) async-start(bf16[128,2,256,128]{2,1,3,0:T(2,128)(2,1)} %stack.2), calls=%async_computation.1 | async-start | bytes 33554432 | tf_op jit(solution)/shard_map/all_to_all | solution.py:17
  49.5 0.1 copy.152
  49.7 0.2 copy.146
  49.9 0.1 split.8
  50.0 0.1 split.9
  50.1 0.1 copy.177
  50.2 0.1 copy.179
  50.5 0.3 fusion.5
  50.7 367.1 %all-to-all-done.1 = bf16[128,2,256,128]{2,1,3,0:T(2,128)(2,1)} async-done(((bf16[128,2,256,128]{2,1,3,0:T(2,128)(2,1)}), bf16[128,2,256,128]{2,1,3,0:T(2,128)(2,1)}, u32[]{:S(2)}, u32[]{:S(2)}) %all-to-all-start.1) | async-done | bytes 16777248 | tf_op jit(solution)/shard_map/all_to_all | solution.py:17
  417.8 14.4 %copy.151 = bf16[128,2,256,128]{2,1,0,3:T(2,128)(2,1)} copy(bf16[128,2,256,128]{2,1,3,0:T(2,128)(2,1)} %all-to-all-done.1) | data formatting | bytes 33554432 | tf_op jit(solution)/shard_map/all_to_all | solution.py:17
  432.2 24.9 %reshape.115 = bf16[256,256,128]{1,0,2:T(8,128)(2,1)} reshape(bf16[128,2,256,128]{2,1,0,3:T(2,128)(2,1)} %copy.151) | data formatting | bytes 33554432 | tf_op jit(solution)/shard_map/reshape | solution.py:18
  457.1 10.2 %fusion.58 = (f32[256,2]{0,1:T(2,128)S(1)}, f32[256,2,128]{0,1,2:T(2,128)S(1)}) fusion(bf16[2,256,128]{1,0,2:T(2,128)(2,1)S(1)} %copy.152, bf16[256,256,128]{1,0,2:T(8,128)(2,1)} %reshape.115), kind=kOutput, calls=%fused_computation.85 | convolution fusion | flops 33619456 | bytes 17172480 | tf_op jit(solution)/shard_map/ikc,jkc->ijc/dot_general | solution.py:117
  467.3 0.2 multiply_reduce_fusion.1
  467.5 0.1 divide_convert_fusion.3
  467.7 0.2 fusion.59
  468.1 0.1 fusion.6
  468.2 0.8 broadcast_in_dim.13
  469.0 10.0 %all-to-all-start.2 = ((bf16[64,4,256,2]{2,1,3,0:T(4,128)(2,1)}), bf16[64,4,256,2]{2,1,3,0:T(4,128)(2,1)S(1)}, u32[]{:S(2)}, u32[]{:S(2)}) async-start(bf16[64,4,256,2]{2,1,3,0:T(4,128)(2,1)} %broadcast_in_dim.13), calls=%async_computation.2 | async-start | bytes 524288 | tf_op jit(solution)/shard_map/all_to_all | solution.py:23
  479.0 0.3 fusion.60
  479.4 0.1 copy.159
  479.6 0.1 copy.160
  479.7 0.1 copy.157
  479.8 0.1 copy.178
  480.0 9.8 %all-to-all-done.2 = bf16[64,4,256,2]{2,1,3,0:T(4,128)(2,1)S(1)} async-done(((bf16[64,4,256,2]{2,1,3,0:T(4,128)(2,1)}), bf16[64,4,256,2]{2,1,3,0:T(4,128)(2,1)S(1)}, u32[]{:S(2)}, u32[]{:S(2)}) %all-to-all-start.2) | async-done | bytes 262176 | tf_op jit(solution)/shard_map/all_to_all | solution.py:23
  489.7 0.1 broadcast_in_dim.14
  489.9 7.3 %all_to_all.33 = bf16[2,64,4,256,2]{3,2,4,1,0:T(4,128)(2,1)S(1)} all-to-all(bf16[2,64,4,256,2]{3,2,4,1,0:T(4,128)(2,1)S(1)} %broadcast_in_dim.14), channel_id=1, replica_groups=mesh['dap_0'=2,'dap_1'=8,'dap_2'=4,'dap_3'=2,'dp'=4] {'dap_3'}, dimensions={0} | all-to-all | bytes 1048576 | tf_op jit(solution)/shard_map/all_to_all | solution.py:23
  497.2 0.1 convert_bitcast_fusion
  497.3 0.6 copy.162
  497.9 0.3 copy.163
  498.2 0.4 copy.164
  498.6 0.9 fusion.61
  499.5 1.1 fusion.11
  500.6 0.1 fusion.30
  500.7 0.2 convolution_add_fusion
  500.9 0.8 copy.167
  (29 shorter events, 0.4 us)
Async XLA Ops:
  0.0 479.0 %copy-start = (bf16[128,512]{1,0:T(8,128)(2,1)S(1)}, bf16[128,512]{1,0:T(8,128)(2,1)}, u32[]{:S(2)}) copy-start(bf16[128,512]{1,0:T(8,128)(2,1)} %param.15) | copy-start | bytes 393220
  0.0 20.7 %copy-start.1 = (bf16[2,256,128]{2,1,0:T(8,128)(2,1)S(1)}, bf16[2,256,128]{2,1,0:T(8,128)(2,1)}, u32[]{:S(2)}) copy-start(bf16[2,256,128]{2,1,0:T(8,128)(2,1)} %param.9) | copy-start | bytes 393220
  0.0 20.7 %copy-start.5 = (bf16[128,256]{1,0:T(8,128)(2,1)S(1)}, bf16[128,256]{1,0:T(8,128)(2,1)}, u32[]{:S(2)}) copy-start(bf16[128,256]{1,0:T(8,128)(2,1)} %param.12) | copy-start | bytes 196612
  3.0 29.3 %all-to-all-start = ((bf16[2,256,129]{2,0,1:T(2,128)(2,1)}), bf16[2,256,129]{2,0,1:T(2,128)(2,1)S(1)}, u32[]{:S(2)}, u32[]{:S(2)}) async-start(bf16[2,256,129]{2,0,1:T(2,128)(2,1)} %pad_maximum_fusion), calls=%async_computation | async-start | bytes 524288 | tf_op jit(solution)/shard_map/all_to_all | solution.py:45
  42.5 7.9 %copy-start.6 = (bf16[128,128]{1,0:T(8,128)(2,1)S(1)}, bf16[128,128]{1,0:T(8,128)(2,1)}, u32[]{:S(2)}) copy-start(bf16[128,128]{1,0:T(8,128)(2,1)} %param.13) | copy-start | bytes 98308
  42.5 375.3 %all-to-all-start.1 = ((bf16[128,2,256,128]{2,1,3,0:T(2,128)(2,1)}), bf16[128,2,256,128]{2,1,3,0:T(2,128)(2,1)}, u32[]{:S(2)}, u32[]{:S(2)}) async-start(bf16[128,2,256,128]{2,1,3,0:T(2,128)(2,1)} %stack.2), calls=%async_computation.1 | async-start | bytes 33554432 | tf_op jit(solution)/shard_map/all_to_all | solution.py:17
  457.1 10.6 %copy-start.2 = (bf16[128,128]{1,0:T(8,128)(2,1)S(1)}, bf16[128,128]{1,0:T(8,128)(2,1)}, u32[]{:S(2)}) copy-start(bf16[128,128]{1,0:T(8,128)(2,1)} %param.14) | copy-start | bytes 98308
  467.3 0.7 copy-start.4
  469.0 20.8 %all-to-all-start.2 = ((bf16[64,4,256,2]{2,1,3,0:T(4,128)(2,1)}), bf16[64,4,256,2]{2,1,3,0:T(4,128)(2,1)S(1)}, u32[]{:S(2)}, u32[]{:S(2)}) async-start(bf16[64,4,256,2]{2,1,3,0:T(4,128)(2,1)} %broadcast_in_dim.13), calls=%async_computation.2 | async-start | bytes 524288 | tf_op jit(solution)/shard_map/all_to_all | solution.py:23
  499.5 1.2 copy-start.3
